TPU v7x, 256 devices: a whole 4x4x8 slice. The times are simulated.
256 devices in a mesh: wide: 64 (over y, x_lo, z), lev: 4 (over x_hi, core).
Axes of the slice: x: 4 (x_hi: 2, x_lo: 2; x = x_hi * 2 + x_lo), y: 4, z: 8, core: 2. Of those that a mesh axis runs over, the one named last changes fastest.
Arguments:
- ensemble: float32 [128, 64, 8192], P(None, 'lev', 'wide'), may hold values from -6 to 6
- innovation: float32 [64, 8192], P('lev', 'wide'), may hold values from -0.4 to 0.4
- obs_inverse: float32 [64, 8192], P('lev', 'wide'), may hold values from 100 to 600
- root_tiles: float32 [8, 128, 128], replicated, may hold values from -0.1875 to 0.1875
- col_index: int32 [64, 8], replicated, may hold values from 0 to 63
- vert_weight: float32 [9, 64], replicated, may hold values from -1 to 1
- member_weight: float32 [128], replicated, may hold values from 0.04 to 0.1
- obs_blocks: int32 [64], replicated, may hold values from 0 to 63
Outputs:
- control: float32 [128, 64, 8192], P(None, 'lev', 'wide')
- increment: float32 [64, 8192], P('lev', 'wide')
Inputs may be any that keep to these rules, and one draw needn't show every extreme that they name: `col_index`: column block numbers; repeats allowed. `obs_blocks`: observed column block numbers; a block listed several times counts that many times.
All inputs are finite; a program needn't handle non-finite values.
Results may differ from a plain program's by a relative error of at most 0.0001.
Values sent between devices are 32-bit elements; how exact they have to be, the bound alone decides.
A program may use at most 128 MiB of HBM per device.

v0:
```python
import jax
import jax.numpy as jnp
from jax import lax
from jax.sharding import PartitionSpec as P


def with_halo(block, sides, width):
    for axis, dim in sides:
        count = lax.axis_size(axis)
        forward = [(i, i + 1) for i in range(count - 1)]
        backward = [(target, source) for source, target in forward]
        low = lax.ppermute(
            lax.slice_in_dim(block, block.shape[dim] - width, None, axis=dim), axis, forward
        )
        high = lax.ppermute(lax.slice_in_dim(block, 0, width, axis=dim), axis, backward)
        block = jnp.concatenate([low, block, high], axis=dim)
    return block


def horizontal(values, root_tiles, col_index):
    slot_count, block_size = (root_tiles.shape[0], root_tiles.shape[1])
    members, levels, columns = values.shape
    row_blocks = columns // block_size
    blocks = values.reshape(members, levels, row_blocks, block_size)
    picked = jnp.take(blocks, col_index.reshape(-1), axis=2)
    picked = picked.reshape(members * levels * row_blocks, slot_count * block_size)
    stacked = root_tiles.reshape(slot_count * block_size, block_size)
    product = jnp.dot(
        picked, stacked, precision=lax.Precision.HIGHEST, preferred_element_type=jnp.float32
    )
    return product.reshape(values.shape)


def horizontal_t(values, root_tiles, col_index):
    slot_count, block_size = (root_tiles.shape[0], root_tiles.shape[1])
    members, levels, columns = values.shape
    row_blocks = columns // block_size
    flat = values.reshape(-1, block_size)
    stacked = jnp.transpose(root_tiles, (2, 0, 1)).reshape(block_size, slot_count * block_size)
    product = jnp.dot(
        flat, stacked, precision=lax.Precision.HIGHEST, preferred_element_type=jnp.float32
    )
    product = product.reshape(members, levels, row_blocks * slot_count, block_size)
    summed = jnp.zeros((members, levels, row_blocks, block_size), jnp.float32)
    summed = summed.at[:, :, col_index.reshape(-1), :].add(product)
    return summed.reshape(values.shape)


def body(
    ensemble, innovation, obs_inverse, root_tiles, col_index, vert_weight, member_weight, obs_blocks
):
    block_size = root_tiles.shape[1]
    lev_dev = ensemble.shape[1]
    col_dev = ensemble.shape[2]
    wide_count = lax.axis_size("wide")
    first_block = lax.axis_index("wide") * (col_dev // block_size)
    block_ids = first_block + jnp.arange(col_dev // block_size, dtype=jnp.int32)
    counts = jnp.sum((obs_blocks[:, None] == block_ids[None, :]).astype(jnp.float32), axis=0)
    obs_weight = obs_inverse * jnp.repeat(counts, block_size)[None, :]
    padded_weights = jnp.pad(vert_weight, ((0, 0), (4, 4)))
    level_start = lax.axis_index("lev") * lev_dev
    wide_weights = lax.dynamic_slice_in_dim(padded_weights, level_start, lev_dev + 8, 1)
    own_weights = wide_weights[:, 4 : 4 + lev_dev]
    weighted = member_weight[:, None, None] * ensemble

    def reverse_items(values):
        blended = horizontal_t(values, root_tiles, col_index)
        padded = with_halo(blended, (("lev", 1),), 4)
        summed = jnp.zeros(values.shape, jnp.float32)
        for offset in range(9):
            lower = 8 - offset
            summed = (
                summed
                + wide_weights[offset, lower : lower + lev_dev][None, :, None]
                * padded[:, lower : lower + lev_dev]
            )
        return summed

    def reverse_grouped(values):
        return reverse_items(values[0])[None]

    def grouped(values):
        return values.reshape(wide_count, values.shape[0] // wide_count, lev_dev, col_dev)

    def adjoint(field_values):
        member_fields = reverse_grouped(
            lax.all_to_all(
                grouped(weighted * field_values[None]),
                "wide",
                split_axis=0,
                concat_axis=3,
                tiled=True,
            )
        )
        return lax.all_to_all(member_fields[0], "wide", split_axis=2, concat_axis=0, tiled=True)

    gradient = adjoint(-(obs_weight * innovation))
    control = jnp.zeros_like(gradient)
    increment = jnp.zeros_like(innovation)
    values = lax.all_to_all(grouped(gradient), "wide", split_axis=0, concat_axis=3, tiled=True)[0]
    padded = with_halo(values, (("lev", 1),), 4)
    blended = jnp.zeros(values.shape, jnp.float32)
    for offset in range(9):
        blended = (
            blended + own_weights[offset][None, :, None] * padded[:, offset : offset + lev_dev]
        )
    mapped = horizontal(blended, root_tiles, col_index)[None]
    by_column = lax.all_to_all(mapped[0], "wide", split_axis=2, concat_axis=0, tiled=True)
    image_field = jnp.sum(weighted * by_column, axis=0)
    grad_norm = lax.psum(jnp.sum(gradient * gradient), ("wide", "lev"))
    gradient_image = gradient + adjoint(obs_weight * image_field)
    curvature = lax.psum(jnp.sum(gradient * gradient_image), ("wide", "lev"))
    step_size = grad_norm / curvature
    control = control - step_size * gradient
    increment = increment - step_size * image_field
    return (control, increment)


def solution(mesh):
    in_specs = (P(None, "lev", "wide"), P("lev", "wide"), P("lev", "wide"), P(), P(), P(), P(), P())
    out_specs = (P(None, "lev", "wide"), P("lev", "wide"))
    return jax.shard_map(body, mesh=mesh, in_specs=in_specs, out_specs=out_specs, check_vma=False)
```

profile of v0, /device:TPU:1, one launch (start us, length us, event | category | flops | bytes accessed | tf_op | source)
XLA Modules:
  0.0 666.0 jit_solution(13129359257538461115)
XLA Ops:
  5.7 13.6 %all-to-all-start = ((f32[64,2,16,128]{3,2,1,0:T(8,128)}), f32[64,2,16,128]{3,2,1,0:T(8,128)S(1)}, u32[]{:S(2)}, u32[]{:S(2)}) async-start(f32[64,2,16,128]{3,2,1,0:T(8,128)} %bitcast.2), calls=%async_computation | async-start | bytes 2097152 | tf_op jit(solution)/shard_map/all_to_all | solution.py:87
  23.1 22.8 %all-to-all-done = f32[64,2,16,128]{3,2,1,0:T(8,128)S(1)} async-done(((f32[64,2,16,128]{3,2,1,0:T(8,128)}), f32[64,2,16,128]{3,2,1,0:T(8,128)S(1)}, u32[]{:S(2)}, u32[]{:S(2)}) %all-to-all-start) | async-done | bytes 1048608 | tf_op jit(solution)/shard_map/all_to_all | solution.py:87
  46.5 8.8 %fusion.54 = f32[2048,1024]{1,0:T(8,128)} fusion(f32[2048,128]{1,0:T(8,128)S(1)} %bitcast.132, f32[128,1024]{0,1:T(8,128)S(1)} %bitcast.120), kind=kOutput, calls=%fused_computation.133 | convolution fusion | flops 3221225472 | bytes 9961472 | tf_op jit(solution)/shard_map/dot_general | solution.py:40
  55.3 9.3 %reshape.144 = f32[2,16,512,128]{3,2,1,0:T(8,128)} reshape(f32[2048,1024]{1,0:T(8,128)} %fusion.54) | data formatting | bytes 16777216 | tf_op jit(solution)/shard_map/reshape | solution.py:43
  64.6 11.4 %copy.67 = f32[2,16,512,128]{3,1,0,2:T(8,128)} copy(f32[2,16,512,128]{3,2,1,0:T(8,128)} %reshape.144) | data formatting | bytes 16777216 | tf_op jit(solution)/shard_map/reshape | solution.py:43
  76.1 50.4 %scatter_fusion = f32[2,16,64,128]{3,1,2,0:T(8,128)S(1)} fusion(f32[2,16,64,128]{3,1,2,0:T(8,128)S(1)} %broadcast.65.clone, s32[512]{0:T(512)S(1)} %bitcast.139, f32[512,2,16,128]{3,2,1,0:T(8,128)} %bitcast.126), kind=kCustom, calls=%fused_computation.1 | custom fusion | flops 2097152 | bytes 25167872 | tf_op jit(solution)/shard_map/scatter-add | solution.py:45
  141.0 7.8 %copy.36 = f32[2,16,8192]{1,0,2:T(2,128)} copy(f32[2,16,8192]{2,1,0:T(8,128)S(1)} %fusion.29) | data formatting | bytes 2097152 | tf_op jit(solution)/shard_map/add | solution.py:73
  148.8 13.2 %reshape.159 = f32[64,1,4096]{2,1,0:T(1,128)S(1)} reshape(f32[8192,2,16]{2,1,0:T(2,128)} %bitcast.127) | data formatting | bytes 2097152
  162.0 31.3 %all_to_all.93 = f32[64,1,4096]{2,1,0:T(1,128)S(1)} all-to-all(f32[64,1,4096]{2,1,0:T(1,128)S(1)} %reshape.159), channel_id=1, replica_groups=mesh['wide'=64,'lev'=4] {'wide'}, dimensions={0} | all-to-all | bytes 2097152 | tf_op jit(solution)/shard_map/all_to_all | solution.py:95
  197.0 12.6 %reshape.160 = f32[8192,2,16]{2,1,0:T(2,128)} reshape(f32[64,4096]{1,0:T(8,128)S(1)} %reduce.4) | data formatting | bytes 2097152
  209.6 10.1 %copy.52 = f32[2,16,64,128]{3,1,0,2:T(8,128)} copy(f32[2,16,64,128]{1,0,3,2:T(2,128)} %bitcast.123) | data formatting | bytes 2097152 | tf_op jit(solution)/shard_map/all_to_all | solution.py:95
  225.8 28.0 %all-to-all-done.2 = f32[64,2,16,128]{3,2,1,0:T(8,128)S(1)} async-done(((f32[64,2,16,128]{3,2,1,0:T(8,128)}), f32[64,2,16,128]{3,2,1,0:T(8,128)S(1)}, u32[]{:S(2)}, u32[]{:S(2)}) %all-to-all-start.2) | async-done | bytes 1048608 | tf_op jit(solution)/shard_map/all_to_all | solution.py:100
  277.9 8.1 %copy.42 = f32[2,16,512,128]{3,2,1,0:T(8,128)} copy(f32[2,16,512,128]{3,1,0,2:T(8,128)S(1)} %select_bitcast_fusion) | data formatting | bytes 16777216 | tf_op jit(solution)/shard_map/jit(_take)/select_n | solution.py:25
  286.0 9.3 %select_n.39 = f32[2048,1024]{1,0:T(8,128)} reshape(f32[2,16,512,128]{3,2,1,0:T(8,128)} %copy.42) | data formatting | bytes 16777216 | tf_op jit(solution)/shard_map/jit(_take)/select_n | solution.py:25
  295.2 9.0 %fusion.55 = f32[2048,128]{1,0:T(8,128)S(1)} fusion(f32[2048,1024]{1,0:T(8,128)} %select_n.39, f32[1024,128]{1,0:T(8,128)S(1)} %bitcast.122), kind=kOutput, calls=%fused_computation.134 | convolution fusion | flops 3221225472 | bytes 9961472 | tf_op jit(solution)/shard_map/dot_general | solution.py:28
  304.5 7.8 %copy.43 = f32[2,16,8192]{1,0,2:T(2,128)} copy(f32[2,16,8192]{2,1,0:T(8,128)S(1)} %squeeze_broadcast_in_dim_reshape.3) | data formatting | bytes 2097152 | tf_op jit(solution)/shard_map/squeeze;broadcast_in_dim;reshape | solution.py:108
  312.3 13.3 %reshape.161 = f32[64,1,4096]{2,1,0:T(1,128)S(1)} reshape(f32[8192,2,16]{2,1,0:T(2,128)} %bitcast.128) | data formatting | bytes 2097152
  325.7 30.9 %all_to_all.94 = f32[64,1,4096]{2,1,0:T(1,128)} all-to-all(f32[64,1,4096]{2,1,0:T(1,128)S(1)} %reshape.161), channel_id=1, replica_groups=mesh['wide'=64,'lev'=4] {'wide'}, dimensions={0} | all-to-all | bytes 2097152 | tf_op jit(solution)/shard_map/all_to_all | solution.py:108
  361.0 12.5 %reshape.162 = f32[8192,2,16]{2,1,0:T(2,128)} reshape(f32[64,4096]{1,0:T(8,128)S(1)} %reduce.5) | data formatting | bytes 2097152
  373.5 9.2 %copy.44 = f32[2,16,64,128]{3,1,0,2:T(8,128)S(1)} copy(f32[2,16,64,128]{1,0,3,2:T(2,128)} %bitcast.129) | data formatting | bytes 2097152 | tf_op jit(solution)/shard_map/all_to_all | solution.py:108
  383.9 33.9 %all_to_all.95 = f32[64,2,16,128]{3,2,1,0:T(8,128)S(1)} all-to-all(f32[64,2,16,128]{3,2,1,0:T(8,128)S(1)} %bitcast.134), channel_id=1, replica_groups=mesh['wide'=64,'lev'=4] {'wide'}, dimensions={0} | all-to-all | bytes 2097152 | tf_op jit(solution)/shard_map/all_to_all | solution.py:87
  418.4 8.8 %fusion.56 = f32[2048,1024]{1,0:T(8,128)} fusion(f32[2048,128]{1,0:T(8,128)S(1)} %bitcast.133, f32[128,1024]{0,1:T(8,128)S(1)} %bitcast.121), kind=kOutput, calls=%fused_computation.135 | convolution fusion | flops 3221225472 | bytes 9961472 | tf_op jit(solution)/shard_map/dot_general | solution.py:40
  427.2 9.3 %reshape.152 = f32[2,16,512,128]{3,2,1,0:T(8,128)} reshape(f32[2048,1024]{1,0:T(8,128)} %fusion.56) | data formatting | bytes 16777216 | tf_op jit(solution)/shard_map/reshape | solution.py:43
  436.5 11.5 %copy.66 = f32[2,16,512,128]{3,1,0,2:T(8,128)} copy(f32[2,16,512,128]{3,2,1,0:T(8,128)} %reshape.152) | data formatting | bytes 16777216 | tf_op jit(solution)/shard_map/reshape | solution.py:43
  448.0 50.4 %scatter_fusion.1 = f32[2,16,64,128]{3,1,2,0:T(8,128)S(1)} fusion(f32[2,16,64,128]{3,1,2,0:T(8,128)S(1)} %broadcast.65, s32[512]{0:T(512)S(1)} %bitcast.141, f32[512,2,16,128]{3,2,1,0:T(8,128)} %bitcast.125), kind=kCustom, calls=%fused_computation.2 | custom fusion | flops 2097152 | bytes 25167872 | tf_op jit(solution)/shard_map/scatter-add | solution.py:45
  510.4 7.8 %copy.48 = f32[2,16,8192]{1,0,2:T(2,128)} copy(f32[2,16,8192]{2,1,0:T(8,128)S(1)} %fusion.4) | data formatting | bytes 2097152 | tf_op jit(solution)/shard_map/add | solution.py:73
  518.2 13.8 %reshape.163 = f32[64,1,4096]{2,1,0:T(1,128)} reshape(f32[8192,2,16]{2,1,0:T(2,128)} %bitcast.130) | data formatting | bytes 2097152
  538.0 6.7 %copy.51 = f32[2,16,64,128]{3,2,1,0:T(8,128)S(1)} copy(f32[2,16,64,128]{1,0,3,2:T(2,128)} %bitcast.124) | data formatting | bytes 2097152 | tf_op jit(solution)/shard_map/all_to_all | solution.py:95
  544.7 18.0 %all-to-all-done.5 = f32[64,1,4096]{2,1,0:T(1,128)} async-done(((f32[64,1,4096]{2,1,0:T(1,128)}), f32[64,1,4096]{2,1,0:T(1,128)}, u32[]{:S(2)}, u32[]{:S(2)}) %all-to-all-start.5) | async-done | bytes 1048608 | tf_op jit(solution)/shard_map/all_to_all | solution.py:95
  567.1 12.6 %reshape.164 = f32[8192,2,16]{2,1,0:T(2,128)} reshape(f32[64,4096]{1,0:T(8,128)S(1)} %reduce.6) | data formatting | bytes 2097152
  579.7 6.7 %copy.53 = f32[2,16,64,128]{3,2,1,0:T(8,128)S(1)} copy(f32[2,16,64,128]{1,0,3,2:T(2,128)} %bitcast.131) | data formatting | bytes 2097152 | tf_op jit(solution)/shard_map/all_to_all | solution.py:95
  587.3 74.6 %all-reduce.1 = (f32[]{:T(128)}, f32[]{:T(128)}) all-reduce(f32[]{:T(128)} %get-tuple-element.3, f32[]{:T(128)} %get-tuple-element.2), channel_id=1, replica_groups=mesh['wide'=64,'lev'=4] {'wide','lev'}, use_global_device_ids=true, to_apply=%region_3.4 | all-reduce | flops 2 | bytes 16 | tf_op jit(solution)/shard_map/psum | solution.py:110
  (68 shorter events, 89.6 us)
Async XLA Ops:
  0.6 45.8 %copy-start = (f32[8,128,128]{2,1,0:T(8,128)S(1)}, f32[8,128,128]{2,1,0:T(8,128)}, u32[]{:S(2)}) copy-start(f32[8,128,128]{2,1,0:T(8,128)} %param.11) | copy-start | bytes 1572868
  5.7 40.1 %all-to-all-start = ((f32[64,2,16,128]{3,2,1,0:T(8,128)}), f32[64,2,16,128]{3,2,1,0:T(8,128)S(1)}, u32[]{:S(2)}, u32[]{:S(2)}) async-start(f32[64,2,16,128]{3,2,1,0:T(8,128)} %bitcast.2), calls=%async_computation | async-start | bytes 2097152 | tf_op jit(solution)/shard_map/all_to_all | solution.py:87
  126.7 11.8 %collective-permute-start = (f32[2,4,8192]{2,1,0:T(4,128)S(1)}, f32[2,4,8192]{2,1,0:T(4,128)S(1)}, u32[]{:S(2)}, u32[]{:S(2)}) collective-permute-start(f32[2,4,8192]{2,1,0:T(4,128)S(1)} %get-tuple-element.10), channel_id=1, source_target_pairs={{1,0},{2,1},{3,2},{5,4},{6,5},{7,6},{9,8},{10,9},{11,10},{13,12},{... | collective-permute-start | bytes 786440 | tf_op jit(solution)/shard_map/ppermute | solution.py:15
  132.1 7.6 %collective-permute-start.1 = (f32[2,4,8192]{2,1,0:T(4,128)S(1)}, f32[2,4,8192]{2,1,0:T(4,128)S(1)}, u32[]{:S(2)}, u32[]{:S(2)}) collective-permute-start(f32[2,4,8192]{2,1,0:T(4,128)S(1)} %get-tuple-element.11), channel_id=1, source_target_pairs={{0,1},{1,2},{2,3},{4,5},{5,6},{6,7},{8,9},{9,10},{10,11},{12,13},{... | collective-permute-start | bytes 786440 | tf_op jit(solution)/shard_map/ppermute | solution.py:12
  219.7 34.1 %all-to-all-start.2 = ((f32[64,2,16,128]{3,2,1,0:T(8,128)}), f32[64,2,16,128]{3,2,1,0:T(8,128)S(1)}, u32[]{:S(2)}, u32[]{:S(2)}) async-start(f32[64,2,16,128]{3,2,1,0:T(8,128)} %bitcast.20), calls=%async_computation.2 | async-start | bytes 2097152 | tf_op jit(solution)/shard_map/all_to_all | solution.py:100
  256.9 9.2 %collective-permute-start.3 = (f32[2,4,8192]{2,1,0:T(4,128)S(1)}, f32[2,4,8192]{2,1,0:T(4,128)S(1)}, u32[]{:S(2)}, u32[]{:S(2)}) collective-permute-start(f32[2,4,8192]{2,1,0:T(4,128)S(1)} %get-tuple-element.8), channel_id=1, source_target_pairs={{1,0},{2,1},{3,2},{5,4},{6,5},{7,6},{9,8},{10,9},{11,10},{13,12},{... | collective-permute-start | bytes 786440 | tf_op jit(solution)/shard_map/ppermute | solution.py:15
  258.9 8.4 %collective-permute-start.2 = (f32[2,4,8192]{2,1,0:T(4,128)S(1)}, f32[2,4,8192]{2,1,0:T(4,128)S(1)}, u32[]{:S(2)}, u32[]{:S(2)}) collective-permute-start(f32[2,4,8192]{2,1,0:T(4,128)S(1)} %get-tuple-element.9), channel_id=1, source_target_pairs={{0,1},{1,2},{2,3},{4,5},{5,6},{6,7},{8,9},{9,10},{10,11},{12,13},{... | collective-permute-start | bytes 786440 | tf_op jit(solution)/shard_map/ppermute | solution.py:12
  361.0 21.8 %copy-start.1 = (f32[128,16,128]{2,1,0:T(8,128)S(1)}, f32[128,16,128]{2,1,0:T(8,128)}, u32[]{:S(2)}) copy-start(f32[128,16,128]{2,1,0:T(8,128)} %param.8) | copy-start | bytes 3145732
  361.0 21.8 %copy-start.3 = (f32[128]{0:T(128)S(1)}, f32[128]{0:T(128)}, u32[]{:S(2)}) copy-start(f32[128]{0:T(128)} %param.14) | copy-start | bytes 1540
  361.0 22.0 %copy-start.2 = (f32[16,128]{1,0:T(8,128)S(1)}, f32[16,128]{1,0:T(8,128)}, u32[]{:S(2)}) copy-start(f32[16,128]{1,0:T(8,128)} %param.10) | copy-start | bytes 24580
  498.6 9.2 %collective-permute-start.4 = (f32[2,4,8192]{2,1,0:T(4,128)S(1)}, f32[2,4,8192]{2,1,0:T(4,128)S(1)}, u32[]{:S(2)}, u32[]{:S(2)}) collective-permute-start(f32[2,4,8192]{2,1,0:T(4,128)S(1)} %get-tuple-element.6), channel_id=1, source_target_pairs={{1,0},{2,1},{3,2},{5,4},{6,5},{7,6},{9,8},{10,9},{11,10},{13,12},{... | collective-permute-start | bytes 786440 | tf_op jit(solution)/shard_map/ppermute | solution.py:15
  500.6 8.4 %collective-permute-start.5 = (f32[2,4,8192]{2,1,0:T(4,128)S(1)}, f32[2,4,8192]{2,1,0:T(4,128)S(1)}, u32[]{:S(2)}, u32[]{:S(2)}) collective-permute-start(f32[2,4,8192]{2,1,0:T(4,128)S(1)} %get-tuple-element.7), channel_id=1, source_target_pairs={{0,1},{1,2},{2,3},{4,5},{5,6},{6,7},{8,9},{9,10},{10,11},{12,13},{... | collective-permute-start | bytes 786440 | tf_op jit(solution)/shard_map/ppermute | solution.py:12
  532.1 30.7 %all-to-all-start.5 = ((f32[64,1,4096]{2,1,0:T(1,128)}), f32[64,1,4096]{2,1,0:T(1,128)}, u32[]{:S(2)}, u32[]{:S(2)}) async-start(f32[64,1,4096]{2,1,0:T(1,128)} %reshape.163), calls=%async_computation.5 | async-start | bytes 2097152 | tf_op jit(solution)/shard_map/all_to_all | solution.py:95
where the time goes:
time: 679 us; the launch traced here: 666 us
  local copies, waits for them, and re-layouts  209 us (31%)
  blocking collectives  171 us (25%)
  other arithmetic  129 us (19%)
  waiting for transfers between devices  78.1 us (12%)
  starting transfers between devices  49.7 us (7%)
  matrix products  26.7 us (4%)
    scatter-add x2, other arithmetic, horizontal_t(): summed = summed.at[:, :, col_index.reshape(-1), :].add(product)  101 us
    unnamed x18, local copies, waits for them, and re-layouts  79 us
    psum x1, blocking collectives, body(): grad_norm = lax.psum(jnp.sum(gradient * gradient), ('wide', 'lev'))  74.6 us
    reshape x4, local copies, waits for them, and re-layouts, horizontal_t(): product.reshape(members, levels, row_blocks * slot_count, block_size)  41.5 us
    all_to_all x1, blocking collectives, adjoint(): lax.all_to_all(grouped(weighted * field_values[None]), 'wide', split_axis...  33.9 us
    all_to_all x1, blocking collectives, adjoint(): lax.all_to_all(member_fields[0], 'wide', split_axis=2, concat_axis=0, til...  31.3 us
    all_to_all x1, blocking collectives, body(): lax.all_to_all(mapped[0], 'wide', split_axis=2, concat_axis=0, tiled=True)  30.9 us
    all_to_all x1, waiting for transfers between devices, body(): lax.all_to_all(grouped(gradient), 'wide', split_axis=0, concat_axis=3, ti...  28 us
  transfers between devices with their start and end apart: 9, of which 9 were waited for; matrix products, arithmetic and copies ran while one was open for 2% of the time, Pallas kernels for 0%

commit v1 on v0

v1 whole, which is shorter than its diff:
```python
import functools

import jax
import jax.numpy as jnp
from jax import lax
from jax.experimental import pallas as pl
from jax.experimental.pallas import tpu as pltpu
from jax.sharding import PartitionSpec as P

MESH = pl.DeviceIdType.MESH
F32 = jnp.float32
BF16 = jnp.bfloat16


def split(value):
    high = value.astype(BF16)
    return high, (value - high.astype(F32)).astype(BF16)


def kernel(
    shape, ens, innov, obsinv, tiles, colt, obs, vw, mw,
    gcol, inc_out, step_out,
    xs, xr, fbuf, gbuf, gs, hbuf, ms, mc, spread, gather, tile_f, tile_b, s_hi, s_lo, mine, slot_a, part, slot_b,
    send, recv,
):
    ny, nz = shape
    wide = ny * 2 * nz
    w = lax.axis_index("wide")
    v = lax.axis_index("lev")
    y, xl, z = w // (2 * nz), (w // nz) % 2, w % nz
    xh, core = v // 2, v % 2
    x = xh * 2 + xl
    me = w * 2 + xh

    def copy(src, dst, phase, w2, v2):
        own = (w2 == w) & (v2 == v)

        @pl.when(own)
        def _():
            pltpu.make_async_copy(src, dst, recv.at[phase]).start()

        @pl.when(jnp.logical_not(own))
        def _():
            pltpu.make_async_remote_copy(
                src_ref=src, dst_ref=dst, send_sem=send.at[phase], recv_sem=recv.at[phase],
                device_id={"wide": w2, "lev": v2}, device_id_type=MESH,
            ).start()

    def arrived(ref, phase):
        pltpu.make_async_copy(ref, ref, recv.at[phase]).wait()

    count = jnp.sum((obs[...] == w).astype(F32), axis=1, keepdims=True)
    weight = obsinv[...] * count
    y0 = -(weight * innov[...])

    def send_x(i, carry):
        z2 = (z + i % nz) % nz
        x2 = (x + (i // nz) % 4) % 4
        y2 = (y + i // (4 * nz)) % ny
        w2 = (y2 * 2 + x2 % 2) * nz + z2
        m = w2 * 2 + x2 // 2
        xs[m] = (mw[m] * ens[m]) * y0
        row = pl.multiple_of(w * 32 + core * 16, 16)
        copy(xs.at[m], xr.at[pl.ds(row, 16)], 0, w2, (x2 // 2) * 2 + xh)
        return carry

    lax.fori_loop(0, 2 * wide, send_x, 0)

    slots = colt.shape[0]
    cols = colt[...]
    two = jnp.concatenate([cols, cols], axis=1)
    fill = jnp.zeros((128 - slots, 128), F32)
    turned = jnp.transpose(
        jnp.concatenate(
            [jnp.pad(cols.astype(F32), ((0, 0), (0, 128 - wide))), fill], axis=0
        )
    )
    row_id = lax.broadcasted_iota(jnp.int32, (wide, 2 * wide), 0)
    lane = lax.broadcasted_iota(jnp.int32, (wide, 2 * wide), 1)
    lane = jnp.where(lane >= wide, lane - wide, lane).astype(F32)
    for j in range(slots):
        spread[j * wide : (j + 1) * wide] = jnp.where(two[j : j + 1] == row_id, 1.0, 0.0).astype(BF16)
        gather[j * wide : (j + 1) * wide] = jnp.where(
            turned[:wide, j : j + 1] == lane, 1.0, 0.0
        ).astype(BF16)
        high, low = split(tiles[j])
        tile_f[j * 128 : (j + 1) * 128] = jnp.concatenate([high, low], axis=1)
        high, low = split(jnp.transpose(tiles[j]))
        tile_b[j * 128 : (j + 1) * 128] = jnp.concatenate([high, low], axis=1)
    zero = jnp.zeros((4, wide, 128), F32)
    for ref in (fbuf, gbuf):
        ref[0:4] = zero
        ref[68:72] = zero

    def horizontal(load, index, table):
        for pair in range(4):
            parts = [split(load(2 * pair + k)) for k in range(2)]
            rhs = jnp.concatenate(
                [jnp.concatenate([p[k] for p in parts], axis=1) for k in range(2)], axis=0
            )
            picked = jnp.dot(index[...], rhs, preferred_element_type=F32)
            for k in range(2):
                at = (2 * pair + k) * wide
                for j in range(slots):
                    high, low = split(picked[j * wide : (j + 1) * wide, k * 128 : (k + 1) * 128])
                    s_hi[at : at + wide, j * 128 : (j + 1) * 128] = high
                    s_lo[at : at + wide, j * 128 : (j + 1) * 128] = low
        first = jnp.dot(s_hi[...], table[...], preferred_element_type=F32)
        second = jnp.dot(s_lo[...], table[:, 0:128], preferred_element_type=F32)
        return first[:, 0:128] + (first[:, 128:256] + second)

    arrived(xr, 0)
    partner = xh * 2 + (1 - core)
    halo = pl.ds(28 + 8 * core, 8)
    halo_copy = pltpu.make_async_remote_copy(
        src_ref=fbuf.at[halo], dst_ref=fbuf.at[halo], send_sem=send.at[1], recv_sem=recv.at[1],
        device_id={"wide": w, "lev": partner}, device_id_type=MESH,
    )

    def spread_group(i, carry):
        group = (1 - core) * (3 - i) + core * i
        out = horizontal(
            lambda k: xr[pl.ds(group * 8 + k, wide, stride=32), :], spread, tile_b
        )
        first = 4 + core * 32 + group * 8
        for k in range(8):
            fbuf[first + k] = out[k * wide : (k + 1) * wide]

        @pl.when(i == 0)
        def _():
            halo_copy.start()

        return carry

    lax.fori_loop(0, 4, spread_group, 0)
    halo_copy.wait()

    def column_g(level):
        total = jnp.zeros((wide, 128), F32)
        for t in range(9):
            at = level - t + 4
            total = total + vw[t, jnp.clip(at, 0, 63)] * fbuf[at + 4]
        return total

    def own_g(i, norm):
        total = column_g(core * 32 + i)
        gbuf[core * 32 + i + 4] = total
        gs[pl.ds(i, wide, stride=32), :] = total
        return norm + total * total

    def send_back(ref, dst, phase, q):
        def one(i, carry):
            z2 = (z + i % nz) % nz
            xl2 = (xl + (i // nz) % 2) % 2
            y2 = (y + i // (2 * nz)) % ny
            w2 = (y2 * 2 + xl2) * nz + z2
            row = pl.multiple_of(w2 * 32 + q * 16, 16)
            copy(ref.at[pl.ds(row, 16)], dst.at[me], phase, w2, 2 * core + q)
            return carry

        lax.fori_loop(0, wide, one, 0)

    norm = lax.fori_loop(0, 32, own_g, jnp.zeros((wide, 128), F32))
    for q in range(2):
        send_back(gs, gcol, 2, q)

    def other_g(i, carry):
        level = 32 - 4 * core + i
        gbuf[level + 4] = column_g(level)
        return carry

    lax.fori_loop(0, 4, other_g, 0)

    def own_h(i, carry):
        level = core * 32 + i
        total = jnp.zeros((wide, 128), F32)
        for t in range(9):
            total = total + vw[t, level] * gbuf[level + t]
        hbuf[i] = total
        return carry

    lax.fori_loop(0, 32, own_h, 0)

    def gather_group(group, carry):
        out = horizontal(lambda k: hbuf[group * 8 + k], gather, tile_f)
        for k in range(8):
            ms[pl.ds(group * 8 + k, wide, stride=32), :] = out[k * wide : (k + 1) * wide]
        return carry

    for q in range(2):
        lax.fori_loop(2 * q, 2 * q + 2, gather_group, 0)
        send_back(ms, mc, 3, q)

    arrived(mc, 3)

    def blend(i, total):
        for k in range(8):
            m = i * 8 + k
            total = total + (mw[m] * ens[m]) * mc[m]
        return total

    image = lax.fori_loop(0, wide // 4, blend, jnp.zeros((16, 128), F32))
    curve = jnp.sum(weight * image * image, axis=0, keepdims=True)
    norm = jnp.sum(norm, axis=0, keepdims=True)
    mine[...] = jnp.concatenate([norm, curve, jnp.zeros((6, 128), F32)], axis=0)

    def share(src, dst, phase, slot, count, target):
        dst[slot] = src[...]
        copies = []
        for i in range(1, count):
            w2, v2 = target((slot + i) % count)
            copies.append(
                pltpu.make_async_remote_copy(
                    src_ref=src, dst_ref=dst.at[slot], send_sem=send.at[phase], recv_sem=recv.at[phase],
                    device_id={"wide": w2, "lev": v2}, device_id_type=MESH,
                )
            )
            copies[-1].start()
        rest = dst.at[pl.ds(0, count - 1)]
        pltpu.make_async_copy(rest, rest, recv.at[phase]).wait()
        return jnp.sum(dst[...], axis=0)

    part[...] = share(
        mine, slot_a, 4, z * 2 + core, 2 * nz,
        lambda s: ((y * 2 + xl) * nz + s // 2, xh * 2 + s % 2),
    )
    total = share(
        part, slot_b, 5, y * 4 + x, 4 * ny,
        lambda s: (((s // 4) * 2 + s % 2) * nz + z, ((s % 4) // 2) * 2 + core),
    )
    norm = jnp.sum(total[0:1], axis=1, keepdims=True)
    curve = jnp.sum(total[1:2], axis=1, keepdims=True)
    step = norm / (norm + curve)
    inc_out[...] = -(step * image)
    step_out[...] = jnp.broadcast_to(-step, (8, 128))

    arrived(gcol, 2)
    for phase, ref, own in ((0, xs, core == xh), (2, gcol, core == xh), (3, mc, core == xh)):

        @pl.when(own)
        def _():
            rest = ref.at[pl.ds(0, 2 * wide - 1)]
            pltpu.make_async_copy(rest, rest, send.at[phase]).wait()

        @pl.when(jnp.logical_not(own))
        def _():
            pltpu.make_async_copy(ref, ref, send.at[phase]).wait()

    for phase, ref, count in ((4, slot_a, 2 * nz), (5, slot_b, 4 * ny)):
        rest = ref.at[pl.ds(0, count - 1)]
        pltpu.make_async_copy(rest, rest, send.at[phase]).wait()


def body(
    shape, ensemble, innovation, obs_inverse, root_tiles, col_index, vert_weight, member_weight, obs_blocks
):
    ny, nz = shape
    wide = ny * 2 * nz
    members, lev, cols = ensemble.shape
    slots = root_tiles.shape[0]
    vmem = pl.BlockSpec(memory_space=pltpu.VMEM)
    smem = pl.BlockSpec(memory_space=pltpu.SMEM)
    v32 = lambda *dims: pltpu.VMEM(dims, F32)
    v16 = lambda *dims: pltpu.VMEM(dims, BF16)
    gradient, increment, scale = pl.pallas_call(
        functools.partial(kernel, shape),
        out_shape=(
            jax.ShapeDtypeStruct(ensemble.shape, F32),
            jax.ShapeDtypeStruct(innovation.shape, F32),
            jax.ShapeDtypeStruct((8, 128), F32),
        ),
        in_specs=[vmem] * 6 + [smem, smem],
        out_specs=(pl.BlockSpec(memory_space=pl.ANY), vmem, vmem),
        scratch_shapes=[
            v32(members, lev, cols),
            v32(wide * 32, 128),
            v32(72, wide, 128),
            v32(72, wide, 128),
            v32(wide * 32, 128),
            v32(32, wide, 128),
            v32(wide * 32, 128),
            v32(members, lev, cols),
            v16(slots * wide, 2 * wide),
            v16(slots * wide, 2 * wide),
            v16(slots * 128, 256),
            v16(slots * 128, 256),
            v16(8 * wide, slots * 128),
            v16(8 * wide, slots * 128),
            v32(8, 128),
            v32(2 * nz, 8, 128),
            v32(8, 128),
            v32(4 * ny, 8, 128),
            pltpu.SemaphoreType.DMA((6,)),
            pltpu.SemaphoreType.DMA((6,)),
        ],
        compiler_params=pltpu.CompilerParams(
            has_side_effects=True, vmem_limit_bytes=48 * 2**20
        ),
    )(
        ensemble,
        innovation,
        obs_inverse,
        root_tiles,
        col_index.T,
        obs_blocks[None],
        vert_weight,
        member_weight,
    )
    return gradient * scale[0, 0], increment


def solution(mesh):
    wide = mesh.shape["wide"]
    nz = min(8, wide // 4)
    shape = (wide // (2 * nz), nz)
    in_specs = (P(None, "lev", "wide"), P("lev", "wide"), P("lev", "wide"), P(), P(), P(), P(), P())
    out_specs = (P(None, "lev", "wide"), P("lev", "wide"))
    return jax.shard_map(
        functools.partial(body, shape), mesh=mesh, in_specs=in_specs, out_specs=out_specs, check_vma=False
    )
```

time: 679 us -> 123 us (0.18); the launches traced: 666 us -> 123 us
  local copies, waits for them, and re-layouts: 209 us -> 6.81 us
  blocking collectives: 171 us -> 0 us
  other arithmetic: 129 us -> 1.68 us
  Pallas kernels: 0 us -> 114 us
  waiting for transfers between devices: 78.1 us -> 0 us
  starting transfers between devices: 49.7 us -> 0 us
  matrix products: 26.7 us -> 0 us
    pallas_call x0 -> x1, Pallas kernels: none -> 114 us  [body(): pl.pallas_call(functools.partial(kernel, shape), out_shape=(jax.ShapeDtyp...]
    scatter-add x2 -> x0, other arithmetic: 101 us -> none  [horizontal_t(): summed = summed.at[:, :, col_index.reshape(-1), :].add(product)]
    all_to_all x3 -> x0, blocking collectives: 96.1 us -> none  [the longest x1 33.9 us: adjoint(): lax.all_to_all(grouped(weighted * field_values[None]), 'wide', split_axis...]
    psum x1 -> x0, blocking collectives: 74.6 us -> none  [body(): grad_norm = lax.psum(jnp.sum(gradient * gradient), ('wide', 'lev'))]
    unnamed x18 -> x17, local copies, waits for them, and re-layouts: 79 us -> 6.29 us
    all_to_all x3 -> x0, waiting for transfers between devices: 68.8 us -> none  [the longest x1 28 us: body(): lax.all_to_all(grouped(gradient), 'wide', split_axis=0, concat_axis=3, ti...]
    reshape x8 -> x0, local copies, waits for them, and re-layouts: 41.8 us -> none  [the longest x4 41.5 us: horizontal_t(): product.reshape(members, levels, row_blocks * slot_count, block_size)]
    all_to_all x8 -> x0, local copies, waits for them, and re-layouts: 36.1 us -> none  [the longest x4 24 us: adjoint(): lax.all_to_all(member_fields[0], 'wide', split_axis=2, concat_axis=0, til...]
  transfers between devices with their start and end apart: 9 -> 0, of which waited for: 9 -> 0; matrix products, arithmetic and copies ran while one was open for 2% -> 0% of each run, Pallas kernels for 0% -> 0%
where the time goes in v1:
time: 123 us
  Pallas kernels  114 us (93%)
  local copies, waits for them, and re-layouts  6.81 us (6%)
  other arithmetic  1.68 us (1%)
    pallas_call x1, Pallas kernels, body(): pl.pallas_call(functools.partial(kernel, shape), out_shape=(jax.ShapeDtyp...  114 us
    unnamed x17, local copies, waits for them, and re-layouts  6.29 us

profile of v1, /device:TPU:1, one launch (start us, length us, event | category | flops | bytes accessed | tf_op | source)
XLA Modules:
  0.0 122.7 jit_solution(2105417126392022627)
XLA Ops:
  0.6 0.0 copy-start.6
  0.6 0.0 copy-start.7
  0.7 0.6 copy-done.6
  1.3 0.0 copy-done.7
  1.3 0.0 copy-start
  1.3 1.2 copy-done
  2.5 0.0 copy-start.1
  2.5 1.0 copy-done.1
  3.6 0.0 copy-start.2
  3.6 0.7 copy-done.2
  4.3 0.0 copy-start.3
  4.3 0.7 copy-done.3
  5.0 0.0 copy-start.4
  5.0 0.7 copy-done.4
  5.7 0.0 copy-start.5
  5.7 0.7 copy-done.5
  6.4 113.6 %shard_map.95 = (f32[128,16,128]{2,1,0:T(8,128)S(1)}, f32[16,128]{1,0:T(8,128)S(1)}, f32[8,128]{1,0:T(8,128)S(1)}) custom-call(f32[128,16,128]{2,1,0:T(8,128)S(1)} %copy-done, f32[16,128]{1,0:T(8,128)S(1)} %copy-done.2, f32[16,128]{1,0:T(8,128)S(1)} %copy-done.3, f32[8,128,128]{2,1,0:T(8,128)S(1)} %copy-done.1, s32[8,64]{1,0:T(8,128)S(1)} %bitcast.3, ...), custom_call_target="tpu_custom_call" | custom-call | tf_op jit(solution)/shard_map/pallas_call | solution.py:265
  119.9 0.5 slice.3
  120.4 1.7 %broadcast_multiply_fusion = f32[128,16,128]{2,1,0:T(8,128)} fusion(f32[128,16,128]{2,1,0:T(8,128)S(1)} %get-tuple-element.5, f32[]{:T(128)} %bitcast.2), kind=kLoop, calls=%fused_computation | loop fusion | flops 262144 | bytes 2097156 | tf_op jit(solution)/shard_map/mul | solution.py:309
  122.1 0.6 copy.11
Async XLA Ops:
  0.6 0.7 copy-start.6
  0.6 0.7 copy-start.7
  1.3 1.2 copy-start
  2.5 1.0 copy-start.1
  3.6 0.7 copy-start.2
  4.3 0.7 copy-start.3
  5.0 0.7 copy-start.4
  5.7 0.7 copy-start.5

commit v2 on v1

v2 whole, which is shorter than its diff:
```python
import functools

import jax
import jax.numpy as jnp
from jax import lax
from jax.experimental import pallas as pl
from jax.experimental.pallas import tpu as pltpu
from jax.sharding import PartitionSpec as P

MESH = pl.DeviceIdType.MESH
F32 = jnp.float32
BF16 = jnp.bfloat16


def split(value):
    high = value.astype(BF16)
    return high, (value - high.astype(F32)).astype(BF16)


def kernel(
    shape, ens, innov, obsinv, tiles_in, colt_in, obs_in, vw, mw, col,
    gcol, image_out, scale_out,
    inn, inv, tiles, colt, obs, zb, yb, xr, fbuf, gbuf, gs, hs, h_hi, h_lo, prod, rp, sz, rz,
    spread, tile_f, tile_b, s_hi, s_lo, mine, slot_a, part, slot_b, load, send, recv, greet,
):
    ny, nz = shape
    wide = ny * 2 * nz
    slots = colt.shape[0]
    w = lax.axis_index("wide")
    v = lax.axis_index("lev")
    y, xl, z = w // (2 * nz), (w // nz) % 2, w % nz
    xh, core = v // 2, v % 2
    x = xh * 2 + xl
    me = w * 2 + xh
    place = (y * 2 + xl) * 2 + core

    def device(y2, x2, z2, core2):
        return {"wide": (y2 * 2 + x2 % 2) * nz + z2, "lev": (x2 // 2) * 2 + core2}

    def near(i):
        s = (z * 2 + core + i) % (2 * nz)
        return device(y, x, s // 2, s % 2)

    def far(i):
        s = (y * 4 + x + i) % (4 * ny)
        return device(s // 4, s % 4, z, core)

    barrier = pltpu.get_barrier_semaphore()
    for i in range(1, 2 * nz):
        pl.semaphore_signal(barrier, inc=1, device_id=near(i), device_id_type=MESH)
    for i in range(1, 4 * ny):
        pl.semaphore_signal(barrier, inc=1, device_id=far(i), device_id_type=MESH)
    loads = [
        pltpu.make_async_copy(src, dst, load.at[i])
        for i, (src, dst) in enumerate(
            ((innov, inn), (obsinv, inv), (obs_in, obs), (colt_in, colt), (tiles_in, tiles))
        )
    ]
    for one in loads:
        one.start()
    pl.semaphore_wait(barrier, 2 * nz + 4 * ny - 2)
    for i in range(1, 4 * ny):
        pl.semaphore_signal(greet.at[0], inc=1, device_id=far(i), device_id_type=MESH)
    for one in loads[:3]:
        one.wait()
    count = jnp.sum((obs[...] == w).astype(F32), axis=1, keepdims=True)
    weight = inv[...] * count
    zb[z] = -(weight * inn[...])
    pl.semaphore_wait(greet.at[0], 4 * ny - 1)

    def remote(src, dst, phase, target):
        pltpu.make_async_remote_copy(
            src_ref=src, dst_ref=dst, send_sem=send.at[phase], recv_sem=recv.at[phase],
            device_id=target, device_id_type=MESH,
        ).start()

    def maybe_own(src, dst, phase, target, own):
        @pl.when(own)
        def _():
            pltpu.make_async_copy(src, dst, recv.at[phase]).start()

        @pl.when(jnp.logical_not(own))
        def _():
            remote(src, dst, phase, target)

    def wait(ref, sem, phase):
        pltpu.make_async_copy(ref, ref, sem.at[phase]).wait()

    for i in range(1, nz):
        remote(zb.at[z], zb.at[z], 0, device(y, x, (z + i) % nz, core))

    def send_x(i):
        z2 = (z + i % nz) % nz
        x2 = (x + (i // nz) % 4) % 4
        y2 = (y + i // (4 * nz)) % ny
        m = ((y2 * 2 + x2 % 2) * nz + z2) * 2 + x2 // 2
        return ens.at[m], xr.at[place, z], 1, device(y2, x2, z2, xh)

    maybe_own(*send_x(0), core == xh)

    def send_x_step(i, carry):
        remote(*send_x(i))
        return carry

    lax.fori_loop(1, wide // 2, send_x_step, 0)

    def send_y0(i):
        return zb, yb.at[place], 2, device((y + i // 4) % ny, (x + i % 4) % 4, z, xh)

    wait(zb.at[pl.ds(0, nz - 1)], recv, 0)
    maybe_own(*send_y0(0), core == xh)
    for i in range(1, 4 * ny):
        remote(*send_y0(i))
    lax.fori_loop(wide // 2, 2 * wide, send_x_step, 0)

    for one in loads[3:]:
        one.wait()
    cols = colt[...]
    two = jnp.concatenate([cols, cols], axis=1)
    row_id = lax.broadcasted_iota(jnp.int32, (wide, 2 * wide), 0)
    for j in range(slots):
        spread[j * wide : (j + 1) * wide] = jnp.where(two[j : j + 1] == row_id, 1.0, 0.0).astype(BF16)

    for j in range(slots):
        high, low = split(tiles[j])
        tile_f[j * 128 : (j + 1) * 128] = jnp.concatenate([high, low], axis=1)
        high, low = split(jnp.transpose(tiles[j]))
        tile_b[j * 128 : (j + 1) * 128] = jnp.concatenate([high, low], axis=1)
    zero = jnp.zeros((4, wide, 128), F32)
    for ref in (fbuf, gbuf):
        ref[0:4] = zero
        ref[68:72] = zero
    own_weight = mw[me]

    def times(table):
        first = jnp.dot(s_hi[...], table[...], preferred_element_type=F32)
        second = jnp.dot(s_lo[...], table[:, 0:128], preferred_element_type=F32)
        return first[:, 0:128] + (first[:, 128:256] + second)

    wait(yb, recv, 2)
    wait(xr, recv, 1)
    partner = device(y, x, z, 1 - core)
    halo = pl.ds(28 + 8 * core, 8)
    halo_copy = pltpu.make_async_remote_copy(
        src_ref=fbuf.at[halo], dst_ref=fbuf.at[halo], send_sem=send.at[4], recv_sem=recv.at[4],
        device_id=partner, device_id_type=MESH,
    )
    xr_rows = xr.reshape(wide * 32, 128)
    yb_rows = yb.reshape(wide * 32, 128)

    def level_x(level):
        parts = []
        for yx in range(2 * ny):
            start = (yx * 2 + level // 16) * nz * 16 + level % 16
            rows = pl.ds(start, nz, stride=16)
            parts.append((own_weight * xr_rows[rows, :]) * yb_rows[rows, :])
        return jnp.concatenate(parts, axis=0)

    def spread_group(i, carry):
        group = (1 - core) * (3 - i) + core * i
        for pair in range(4):
            parts = [split(level_x(group * 8 + 2 * pair + k)) for k in range(2)]
            rhs = jnp.concatenate(
                [jnp.concatenate([p[k] for p in parts], axis=1) for k in range(2)], axis=0
            )
            picked = jnp.dot(spread[...], rhs, preferred_element_type=F32)
            for k in range(2):
                at = (2 * pair + k) * wide
                for j in range(slots):
                    high, low = split(picked[j * wide : (j + 1) * wide, k * 128 : (k + 1) * 128])
                    s_hi[at : at + wide, j * 128 : (j + 1) * 128] = high
                    s_lo[at : at + wide, j * 128 : (j + 1) * 128] = low
        out = times(tile_b)
        first = 4 + core * 32 + group * 8
        for k in range(8):
            fbuf[first + k] = out[k * wide : (k + 1) * wide]

        @pl.when(i == 0)
        def _():
            halo_copy.start()

        return carry

    lax.fori_loop(0, 4, spread_group, 0)
    halo_copy.wait()

    def column_g(level):
        total = jnp.zeros((wide, 128), F32)
        for t in range(9):
            at = level - t + 4
            total = total + vw[t, jnp.clip(at, 0, 63)] * fbuf[at + 4]
        return total

    def own_g(i, norm):
        total = column_g(core * 32 + i)
        gbuf[core * 32 + i + 4] = total
        gs[pl.ds(i, wide, stride=32), :] = total
        return norm + total * total

    norm = lax.fori_loop(0, 32, own_g, jnp.zeros((wide, 128), F32))

    def send_g(i):
        q = (core + i % 2) % 2
        z2 = (z + (i // 2) % nz) % nz
        xl2 = (xl + (i // (2 * nz)) % 2) % 2
        y2 = (y + i // (4 * nz)) % ny
        w2 = (y2 * 2 + xl2) * nz + z2
        row = pl.multiple_of(w2 * 32 + q * 16, 16)
        return gs.at[pl.ds(row, 16)], gcol.at[me], 5, {"wide": w2, "lev": 2 * core + q}

    maybe_own(*send_g(0), core == xh)

    def send_g_step(i, carry):
        remote(*send_g(i))
        return carry

    lax.fori_loop(1, wide // 4, send_g_step, 0)

    def other_g(i, carry):
        level = 32 - 4 * core + i
        gbuf[level + 4] = column_g(level)
        return carry

    lax.fori_loop(0, 4, other_g, 0)

    def own_h(i, carry):
        level = core * 32 + i
        total = jnp.zeros((wide, 128), F32)
        for t in range(9):
            total = total + vw[t, level] * gbuf[level + t]
        hs[pl.ds(i, wide, stride=32), :] = total
        return carry

    lax.fori_loop(0, 32, own_h, 0)

    def cut(b, carry):
        high, low = split(hs[pl.ds(pl.multiple_of(b * 32, 32), 32), :])
        h_hi[b] = high
        h_lo[b] = low
        return carry

    lax.fori_loop(0, wide, cut, 0)

    def gather_y(y2):
        for r in range(2 * nz):
            for j in range(slots):
                source = col[j, y2 * 2 * nz + r]
                s_hi[r * 32 : (r + 1) * 32, j * 128 : (j + 1) * 128] = h_hi[source]
                s_lo[r * 32 : (r + 1) * 32, j * 128 : (j + 1) * 128] = h_lo[source]
        out = times(tile_f)
        for r in range(2 * nz):
            for q in range(2):
                at = r * 32 + q * 16
                to = y2 * 4 + (r // nz) * 2 + q
                prod[to, r % nz] = (own_weight * xr[to, r % nz]) * out[at : at + 16]

    def send_p(y2, i):
        q = (core + i % 2) % 2
        xl2 = (xl + i // 2) % 2
        return prod.at[y2 * 4 + xl2 * 2 + q], rp.at[y * 4 + x], 6, device(y2, core * 2 + xl2, z, q)

    done = wide // 4
    more = (2 * wide - done) // ny

    def gather_step(i, carry):
        y2 = (y + 1 + i) % ny
        gather_y(y2)
        for k in range(4):
            remote(*send_p(y2, k))
        lax.fori_loop(done + i * more, done + (i + 1) * more, send_g_step, 0)
        return carry

    lax.fori_loop(0, ny - 1, gather_step, 0)
    gather_y(y)
    maybe_own(*send_p(y, 0), core == xh)
    for k in range(1, 4):
        remote(*send_p(y, k))
    lax.fori_loop(done + (ny - 1) * more, 2 * wide, send_g_step, 0)
    wait(rp, recv, 6)
    total = rp[0]
    for k in range(1, 4 * ny):
        total = total + rp[k]
    sz[...] = total
    for i in range(1, nz):
        remote(sz.at[(z + i) % nz], rz.at[z], 8, device(y, x, (z + i) % nz, core))
    rz[z] = sz[z]
    wait(rz.at[pl.ds(0, nz - 1)], recv, 8)
    image = rz[0]
    for k in range(1, nz):
        image = image + rz[k]
    image_out[...] = image

    curve = jnp.sum(weight * image * image, axis=0, keepdims=True)
    norm = jnp.sum(norm, axis=0, keepdims=True)
    mine[...] = jnp.concatenate([norm, curve, jnp.zeros((6, 128), F32)], axis=0)

    def share(src, dst, phase, slot, count, target):
        for i in range(1, count):
            remote(src, dst.at[slot], phase, target(i))
        dst[slot] = src[...]
        wait(dst.at[pl.ds(0, count - 1)], recv, phase)
        total = dst[0]
        for k in range(1, count):
            total = total + dst[k]
        return total

    part[...] = share(mine, slot_a, 9, z * 2 + core, 2 * nz, near)
    total = share(part, slot_b, 10, y * 4 + x, 4 * ny, far)
    norm = jnp.sum(total[0:1], axis=1, keepdims=True)
    curve = jnp.sum(total[1:2], axis=1, keepdims=True)
    scale_out[...] = jnp.broadcast_to(-(norm / (norm + curve)), (16, 128))

    wait(gcol, recv, 5)
    some = 2 * wide - 1
    for phase, all_of, but_one in (
        (1, gcol, gcol.at[pl.ds(0, some)]),
        (2, yb, yb.at[pl.ds(0, 4 * ny - 1)]),
        (5, gcol, gcol.at[pl.ds(0, some)]),
        (6, rp, rp.at[pl.ds(0, 4 * ny - 1)]),
    ):

        @pl.when(core == xh)
        def _():
            wait(but_one, send, phase)

        @pl.when(core != xh)
        def _():
            wait(all_of, send, phase)

    for phase, ref, count in (
        (0, zb, nz - 1), (8, rz, nz - 1), (9, slot_a, 2 * nz - 1), (10, slot_b, 4 * ny - 1)
    ):
        wait(ref.at[pl.ds(0, count)], send, phase)


def body(
    shape, ensemble, innovation, obs_inverse, root_tiles, col_index, vert_weight, member_weight, obs_blocks
):
    ny, nz = shape
    wide = ny * 2 * nz
    lev, cols = innovation.shape
    slots = root_tiles.shape[0]
    vmem = pl.BlockSpec(memory_space=pltpu.VMEM)
    smem = pl.BlockSpec(memory_space=pltpu.SMEM)
    hbm = pl.BlockSpec(memory_space=pl.ANY)
    v32 = lambda *dims: pltpu.VMEM(dims, F32)
    v16 = lambda *dims: pltpu.VMEM(dims, BF16)
    group = max(8 * wide, 2 * nz * 32)
    gradient, image, scale = pl.pallas_call(
        functools.partial(kernel, shape),
        out_shape=(
            jax.ShapeDtypeStruct(ensemble.shape, F32),
            jax.ShapeDtypeStruct(innovation.shape, F32),
            jax.ShapeDtypeStruct(innovation.shape, F32),
        ),
        in_specs=[hbm] * 6 + [smem] * 3,
        out_specs=(hbm, vmem, vmem),
        scratch_shapes=[
            v32(lev, cols),
            v32(lev, cols),
            v32(*root_tiles.shape),
            pltpu.VMEM((slots, wide), jnp.int32),
            pltpu.VMEM((1, obs_blocks.shape[0]), jnp.int32),
            v32(nz, 16, 128),
            v32(4 * ny, nz, 16, 128),
            v32(4 * ny, nz, 16, 128),
            v32(72, wide, 128),
            v32(72, wide, 128),
            v32(wide * 32, 128),
            v32(wide * 32, 128),
            v16(wide, 32, 128),
            v16(wide, 32, 128),
            v32(4 * ny, nz, 16, 128),
            v32(4 * ny, nz, 16, 128),
            v32(nz, 16, 128),
            v32(nz, 16, 128),
            v16(slots * wide, 2 * wide),
            v16(slots * 128, 256),
            v16(slots * 128, 256),
            v16(group, slots * 128),
            v16(group, slots * 128),
            v32(8, 128),
            v32(2 * nz, 8, 128),
            v32(8, 128),
            v32(4 * ny, 8, 128),
            pltpu.SemaphoreType.DMA((5,)),
            pltpu.SemaphoreType.DMA((11,)),
            pltpu.SemaphoreType.DMA((11,)),
            pltpu.SemaphoreType.REGULAR((1,)),
        ],
        compiler_params=pltpu.CompilerParams(
            has_side_effects=True, collective_id=0, vmem_limit_bytes=62 * 2**20
        ),
    )(
        ensemble,
        innovation,
        obs_inverse,
        root_tiles,
        col_index.T,
        obs_blocks[None],
        vert_weight,
        member_weight,
        col_index.T,
    )
    return gradient * scale[None], image * scale


def solution(mesh):
    wide = mesh.shape["wide"]
    nz = 8 if wide % 16 == 0 else 2
    shape = (wide // (2 * nz), nz)
    in_specs = (P(None, "lev", "wide"), P("lev", "wide"), P("lev", "wide"), P(), P(), P(), P(), P())
    out_specs = (P(None, "lev", "wide"), P("lev", "wide"))
    return jax.shard_map(
        functools.partial(body, shape), mesh=mesh, in_specs=in_specs, out_specs=out_specs, check_vma=False
    )
```

time: 123 us -> 110 us (0.89)
  Pallas kernels: 114 us -> 106 us
  local copies, waits for them, and re-layouts: 6.81 us -> 0.01 us
    pallas_call x1, Pallas kernels: 114 us -> 106 us  [body(): pl.pallas_call(functools.partial(kernel, shape), out_shape=(jax.ShapeDtyp...]
    unnamed x17 -> x4, local copies, waits for them, and re-layouts: 6.29 us -> 0.01 us
    mul x1 -> x2, other arithmetic: 1.68 us -> 2.88 us  [body(): return (gradient * scale[None], image * scale)]
where the time goes in v2:
time: 110 us
  Pallas kernels  106 us (96%)
  other arithmetic  2.88 us (3%)
    pallas_call x1, Pallas kernels, body(): pl.pallas_call(functools.partial(kernel, shape), out_shape=(jax.ShapeDtyp...  106 us
    mul x2, other arithmetic, body(): return (gradient * scale[None], image * scale)  2.88 us

profile of v2, /device:TPU:1, one launch (start us, length us, event | category | flops | bytes accessed | tf_op | source)
XLA Modules:
  0.0 109.9 jit_solution(8345649352063895953)
XLA Ops:
  0.6 106.3 %shard_map.95 = (f32[128,16,128]{2,1,0:T(8,128)}, f32[16,128]{1,0:T(8,128)}, f32[16,128]{1,0:T(8,128)}) custom-call(f32[128,16,128]{2,1,0:T(8,128)} %ens.1, f32[16,128]{1,0:T(8,128)} %innov.1, f32[16,128]{1,0:T(8,128)} %obsinv.1, f32[8,128,128]{2,1,0:T(8,128)} %tiles_in.1, s32[8,64]{1,0:T(8,128)} %bitcast.2, s32[1,64]{1,0:T(1,128)} %bitcast.4, f32[9,64]{1,0:T(8,128)} %vw.1, ...), custom_call_target="tpu_custom_call" | custom-call | tf_op jit(solution)/shard_map/pallas_call | solution.py:349
  107.0 0.0 copy-start
  107.0 0.0 copy-start.1
  107.0 2.3 %broadcast_multiply_fusion = f32[128,16,128]{2,1,0:T(8,128)} fusion(f32[128,16,128]{2,1,0:T(8,128)} %get-tuple-element.5, f32[16,128]{1,0:T(8,128)} %get-tuple-element.6), kind=kLoop, calls=%fused_computation | loop fusion | flops 262144 | bytes 2105344 | tf_op jit(solution)/shard_map/mul | solution.py:405
  109.3 0.0 copy-done
  109.3 0.0 copy-done.1
  109.3 0.6 mul.13
Async XLA Ops:
  107.0 2.3 %copy-start = (f32[16,128]{1,0:T(8,128)S(1)}, f32[16,128]{1,0:T(8,128)}, u32[]{:S(2)}) copy-start(f32[16,128]{1,0:T(8,128)} %get-tuple-element.6) | copy-start | bytes 24580
  107.0 2.3 %copy-start.1 = (f32[16,128]{1,0:T(8,128)S(1)}, f32[16,128]{1,0:T(8,128)}, u32[]{:S(2)}) copy-start(f32[16,128]{1,0:T(8,128)} %get-tuple-element.7) | copy-start | bytes 24580

commit v3 on v2

--- a/solution.py
+++ b/solution.py
@@ -20,7 +20,7 @@
 def kernel(
     shape, ens, innov, obsinv, tiles_in, colt_in, obs_in, vw, mw, col,
     gcol, image_out, scale_out,
-    inn, inv, tiles, colt, obs, zb, yb, xr, fbuf, gbuf, gs, hs, h_hi, h_lo, prod, rp, sz, rz,
+    inn, inv, tiles, colt, obs, zb, yb, xr, fbuf, gbuf, gs, tz, hs, h_hi, h_lo, prod, rp, sz, rz,
     spread, tile_f, tile_b, s_hi, s_lo, mine, slot_a, part, slot_b, load, send, recv, greet,
 ):
     ny, nz = shape
@@ -142,7 +142,7 @@
     partner = device(y, x, z, 1 - core)
     halo = pl.ds(28 + 8 * core, 8)
     halo_copy = pltpu.make_async_remote_copy(
-        src_ref=fbuf.at[halo], dst_ref=fbuf.at[halo], send_sem=send.at[4], recv_sem=recv.at[4],
+        src_ref=fbuf.at[halo], dst_ref=fbuf.at[halo], send_sem=send.at[7], recv_sem=recv.at[7],
         device_id=partner, device_id_type=MESH,
     )
     xr_rows = xr.reshape(wide * 32, 128)
@@ -191,30 +191,39 @@
             total = total + vw[t, jnp.clip(at, 0, 63)] * fbuf[at + 4]
         return total
 
+    gs_rows = gs.reshape(wide * 32, 128)
+
     def own_g(i, norm):
         total = column_g(core * 32 + i)
         gbuf[core * 32 + i + 4] = total
-        gs[pl.ds(i, wide, stride=32), :] = total
+        gs_rows[pl.ds(i, wide, stride=32), :] = total
         return norm + total * total
 
-    norm = lax.fori_loop(0, 32, own_g, jnp.zeros((wide, 128), F32))
-
-    def send_g(i):
-        q = (core + i % 2) % 2
-        z2 = (z + (i // 2) % nz) % nz
-        xl2 = (xl + (i // (2 * nz)) % 2) % 2
-        y2 = (y + i // (4 * nz)) % ny
-        w2 = (y2 * 2 + xl2) * nz + z2
-        row = pl.multiple_of(w2 * 32 + q * 16, 16)
-        return gs.at[pl.ds(row, 16)], gcol.at[me], 5, {"wide": w2, "lev": 2 * core + q}
-
-    maybe_own(*send_g(0), core == xh)
-
-    def send_g_step(i, carry):
-        remote(*send_g(i))
-        return carry
-
-    lax.fori_loop(1, wide // 4, send_g_step, 0)
+
+    def along_z(q):
+        half = pl.ds(16 * q, 16)
+        pltpu.make_async_copy(gs.at[:, z, half], tz.at[q, :, z], recv.at[3 + q]).start()
+        for i in range(1, nz):
+            z2 = (z + i) % nz
+            remote(gs.at[:, z2, half], tz.at[q, :, z], 3 + q, device(y, x, z2, core))
+
+    def within(q):
+        wait(tz.at[q], recv, 3 + q)
+        first = pl.ds((y * 2 + xl) * nz, nz)
+        for i in range(2 * ny):
+            y2 = (y + i // 2) % ny
+            xl2 = (xl + i % 2) % 2
+            target = device(y2, core * 2 + xl2, z, q)
+            args = (tz.at[q, y2 * 2 + xl2], gcol.at[first, xh], 5, target)
+            if i:
+                remote(*args)
+            else:
+                maybe_own(*args, (core == xh) & (core == q))
+
+    norm = lax.fori_loop(0, 16, own_g, jnp.zeros((wide, 128), F32))
+    along_z(0)
+    norm = lax.fori_loop(16, 32, own_g, norm)
+    along_z(1)
 
     def other_g(i, carry):
         level = 32 - 4 * core + i
@@ -259,15 +268,11 @@
         xl2 = (xl + i // 2) % 2
         return prod.at[y2 * 4 + xl2 * 2 + q], rp.at[y * 4 + x], 6, device(y2, core * 2 + xl2, z, q)
 
-    done = wide // 4
-    more = (2 * wide - done) // ny
-
     def gather_step(i, carry):
         y2 = (y + 1 + i) % ny
         gather_y(y2)
         for k in range(4):
             remote(*send_p(y2, k))
-        lax.fori_loop(done + i * more, done + (i + 1) * more, send_g_step, 0)
         return carry
 
     lax.fori_loop(0, ny - 1, gather_step, 0)
@@ -275,7 +280,7 @@
     maybe_own(*send_p(y, 0), core == xh)
     for k in range(1, 4):
         remote(*send_p(y, k))
-    lax.fori_loop(done + (ny - 1) * more, 2 * wide, send_g_step, 0)
+    within(0)
     wait(rp, recv, 6)
     total = rp[0]
     for k in range(1, 4 * ny):
@@ -294,17 +299,19 @@
     norm = jnp.sum(norm, axis=0, keepdims=True)
     mine[...] = jnp.concatenate([norm, curve, jnp.zeros((6, 128), F32)], axis=0)
 
-    def share(src, dst, phase, slot, count, target):
+    def share(src, dst, phase, slot, count, target, beside=None):
         for i in range(1, count):
             remote(src, dst.at[slot], phase, target(i))
         dst[slot] = src[...]
+        if beside:
+            beside()
         wait(dst.at[pl.ds(0, count - 1)], recv, phase)
         total = dst[0]
         for k in range(1, count):
             total = total + dst[k]
         return total
 
-    part[...] = share(mine, slot_a, 9, z * 2 + core, 2 * nz, near)
+    part[...] = share(mine, slot_a, 9, z * 2 + core, 2 * nz, near, functools.partial(within, 1))
     total = share(part, slot_b, 10, y * 4 + x, 4 * ny, far)
     norm = jnp.sum(total[0:1], axis=1, keepdims=True)
     curve = jnp.sum(total[1:2], axis=1, keepdims=True)
@@ -312,10 +319,11 @@
 
     wait(gcol, recv, 5)
     some = 2 * wide - 1
+    xs_all = xr.reshape(2 * wide, 16, 128)
     for phase, all_of, but_one in (
-        (1, gcol, gcol.at[pl.ds(0, some)]),
+        (1, xs_all, xs_all.at[pl.ds(0, some)]),
         (2, yb, yb.at[pl.ds(0, 4 * ny - 1)]),
-        (5, gcol, gcol.at[pl.ds(0, some)]),
+        (5, rp, rp.at[pl.ds(0, 4 * ny - 1)]),
         (6, rp, rp.at[pl.ds(0, 4 * ny - 1)]),
     ):
 
@@ -328,7 +336,7 @@
             wait(all_of, send, phase)
 
     for phase, ref, count in (
-        (0, zb, nz - 1), (8, rz, nz - 1), (9, slot_a, 2 * nz - 1), (10, slot_b, 4 * ny - 1)
+        (0, zb, nz - 1), (3, rp, nz - 1), (4, rp, nz - 1), (8, rz, nz - 1), (9, slot_a, 2 * nz - 1), (10, slot_b, 4 * ny - 1)
     ):
         wait(ref.at[pl.ds(0, count)], send, phase)
 
@@ -349,7 +357,7 @@
     gradient, image, scale = pl.pallas_call(
         functools.partial(kernel, shape),
         out_shape=(
-            jax.ShapeDtypeStruct(ensemble.shape, F32),
+            jax.ShapeDtypeStruct((wide, 2, lev, cols), F32),
             jax.ShapeDtypeStruct(innovation.shape, F32),
             jax.ShapeDtypeStruct(innovation.shape, F32),
         ),
@@ -366,7 +374,8 @@
             v32(4 * ny, nz, 16, 128),
             v32(72, wide, 128),
             v32(72, wide, 128),
-            v32(wide * 32, 128),
+            v32(2 * ny, nz, 32, 128),
+            v32(2, 2 * ny, nz, 16, 128),
             v32(wide * 32, 128),
             v16(wide, 32, 128),
             v16(wide, 32, 128),
@@ -402,7 +411,7 @@
         member_weight,
         col_index.T,
     )
-    return gradient * scale[None], image * scale
+    return (gradient * scale).reshape(ensemble.shape), image * scale
 
 
 def solution(mesh):

time: 110 us -> 96.4 us (0.88)
  Pallas kernels: 106 us -> 92.7 us
    pallas_call x1, Pallas kernels: 106 us -> 92.7 us  [body(): pl.pallas_call(functools.partial(kernel, shape), out_shape=(jax.ShapeDtyp...]
where the time goes in v3:
time: 96.4 us; the launch traced here: 96.3 us
  Pallas kernels  92.7 us (96%)
  other arithmetic  2.9 us (3%)
    pallas_call x1, Pallas kernels, body(): pl.pallas_call(functools.partial(kernel, shape), out_shape=(jax.ShapeDtyp...  92.7 us
    mul x2, other arithmetic, body(): return ((gradient * scale).reshape(ensemble.shape), image * scale)  2.9 us

profile of v3, /device:TPU:1, one launch (start us, length us, event | category | flops | bytes accessed | tf_op | source)
XLA Modules:
  0.0 96.3 jit_solution(1301337122931816480)
XLA Ops:
  0.6 92.7 %shard_map.95 = (f32[64,2,16,128]{3,2,1,0:T(8,128)}, f32[16,128]{1,0:T(8,128)}, f32[16,128]{1,0:T(8,128)}) custom-call(f32[128,16,128]{2,1,0:T(8,128)} %ens.1, f32[16,128]{1,0:T(8,128)} %innov.1, f32[16,128]{1,0:T(8,128)} %obsinv.1, f32[8,128,128]{2,1,0:T(8,128)} %tiles_in.1, s32[8,64]{1,0:T(8,128)} %bitcast.4, s32[1,64]{1,0:T(1,128)} %bitcast.6, ...), custom_call_target="tpu_custom_call" | custom-call | tf_op jit(solution)/shard_map/pallas_call | solution.py:357
  93.3 0.0 copy-start
  93.4 0.0 copy-start.1
  93.4 2.3 %broadcast_multiply_fusion = f32[64,2,16,128]{3,2,1,0:T(8,128)} fusion(f32[64,2,16,128]{3,2,1,0:T(8,128)} %get-tuple-element.5, f32[16,128]{1,0:T(8,128)} %get-tuple-element.6), kind=kLoop, calls=%fused_computation | loop fusion | flops 262144 | bytes 2105344 | tf_op jit(solution)/shard_map/mul | solution.py:414
  95.7 0.0 copy-done
  95.7 0.0 copy-done.1
  95.7 0.6 mul.13
Async XLA Ops:
  93.3 2.3 %copy-start = (f32[16,128]{1,0:T(8,128)S(1)}, f32[16,128]{1,0:T(8,128)}, u32[]{:S(2)}) copy-start(f32[16,128]{1,0:T(8,128)} %get-tuple-element.6) | copy-start | bytes 24580
  93.4 2.3 %copy-start.1 = (f32[16,128]{1,0:T(8,128)S(1)}, f32[16,128]{1,0:T(8,128)}, u32[]{:S(2)}) copy-start(f32[16,128]{1,0:T(8,128)} %get-tuple-element.7) | copy-start | bytes 24580

commit v4 on v3

--- a/solution.py
+++ b/solution.py
@@ -20,8 +20,8 @@
 def kernel(
     shape, ens, innov, obsinv, tiles_in, colt_in, obs_in, vw, mw, col,
     gcol, image_out, scale_out,
-    inn, inv, tiles, colt, obs, zb, yb, xr, fbuf, gbuf, gs, tz, hs, h_hi, h_lo, prod, rp, sz, rz,
-    spread, tile_f, tile_b, s_hi, s_lo, mine, slot_a, part, slot_b, load, send, recv, greet,
+    inn, inv, tiles, colt, obs, zb, yb, xr, fbuf, gbuf, gs, tz, tq, hs, h_hi, h_lo, prod, rp, sz, rz,
+    spread, tile_f, tile_b, s_hi, s_lo, mine, slot_a, part, slot_b, load, send, recv,
 ):
     ny, nz = shape
     wide = ny * 2 * nz
@@ -45,11 +45,33 @@
         s = (y * 4 + x + i) % (4 * ny)
         return device(s // 4, s % 4, z, core)
 
+    def remote(src, dst, phase, target, sent=None):
+        pltpu.make_async_remote_copy(
+            src_ref=src, dst_ref=dst, send_sem=send.at[phase if sent is None else sent], recv_sem=recv.at[phase],
+            device_id=target, device_id_type=MESH,
+        ).start()
+
+    def maybe_own(src, dst, phase, target, own, sent=None):
+        @pl.when(own)
+        def _():
+            pltpu.make_async_copy(src, dst, recv.at[phase]).start()
+
+        @pl.when(jnp.logical_not(own))
+        def _():
+            remote(src, dst, phase, target, sent)
+
+    def wait(ref, sem, phase):
+        pltpu.make_async_copy(ref, ref, sem.at[phase]).wait()
+
+    def plane(i):
+        s = ((y * 4 + x) * 2 + core + i) % (8 * ny)
+        return device(s // 8, (s // 2) % 4, z, s % 2)
+
     barrier = pltpu.get_barrier_semaphore()
     for i in range(1, 2 * nz):
         pl.semaphore_signal(barrier, inc=1, device_id=near(i), device_id_type=MESH)
-    for i in range(1, 4 * ny):
-        pl.semaphore_signal(barrier, inc=1, device_id=far(i), device_id_type=MESH)
+    for i in range(1, 8 * ny):
+        pl.semaphore_signal(barrier, inc=1, device_id=plane(i), device_id_type=MESH)
     loads = [
         pltpu.make_async_copy(src, dst, load.at[i])
         for i, (src, dst) in enumerate(
@@ -58,51 +80,28 @@
     ]
     for one in loads:
         one.start()
-    pl.semaphore_wait(barrier, 2 * nz + 4 * ny - 2)
-    for i in range(1, 4 * ny):
-        pl.semaphore_signal(greet.at[0], inc=1, device_id=far(i), device_id_type=MESH)
+    pl.semaphore_wait(barrier, 2 * nz + 8 * ny - 2)
     for one in loads[:3]:
         one.wait()
     count = jnp.sum((obs[...] == w).astype(F32), axis=1, keepdims=True)
     weight = inv[...] * count
     zb[z] = -(weight * inn[...])
-    pl.semaphore_wait(greet.at[0], 4 * ny - 1)
-
-    def remote(src, dst, phase, target):
-        pltpu.make_async_remote_copy(
-            src_ref=src, dst_ref=dst, send_sem=send.at[phase], recv_sem=recv.at[phase],
-            device_id=target, device_id_type=MESH,
-        ).start()
-
-    def maybe_own(src, dst, phase, target, own):
-        @pl.when(own)
-        def _():
-            pltpu.make_async_copy(src, dst, recv.at[phase]).start()
-
-        @pl.when(jnp.logical_not(own))
-        def _():
-            remote(src, dst, phase, target)
-
-    def wait(ref, sem, phase):
-        pltpu.make_async_copy(ref, ref, sem.at[phase]).wait()
 
     for i in range(1, nz):
         remote(zb.at[z], zb.at[z], 0, device(y, x, (z + i) % nz, core))
 
-    def send_x(i):
-        z2 = (z + i % nz) % nz
-        x2 = (x + (i // nz) % 4) % 4
-        y2 = (y + i // (4 * nz)) % ny
-        m = ((y2 * 2 + x2 % 2) * nz + z2) * 2 + x2 // 2
-        return ens.at[m], xr.at[place, z], 1, device(y2, x2, z2, xh)
-
-    maybe_own(*send_x(0), core == xh)
-
-    def send_x_step(i, carry):
-        remote(*send_x(i))
-        return carry
-
-    lax.fori_loop(1, wide // 2, send_x_step, 0)
+    pieces = []
+    for late in range(2):
+        rows = pl.ds(pl.multiple_of(8 * ((1 - xh) * (1 - late) + xh * late), 8), 8)
+        for dy in range(ny):
+            pieces.append((late, dy, rows))
+
+    for p, (late, dy, rows) in enumerate(pieces):
+        y2 = pl.ds(2 * ((y + dy) % ny), 2)
+        pltpu.make_async_copy(ens.at[y2, z, :, rows], tq.at[p, :, :, z], recv.at[14 + p]).start()
+        for i in range(1, nz):
+            z2 = (z + i) % nz
+            remote(ens.at[y2, z2, :, rows], tq.at[p, :, :, z], 14 + p, device(y, x, z2, core), 12)
 
     def send_y0(i):
         return zb, yb.at[place], 2, device((y + i // 4) % ny, (x + i % 4) % 4, z, xh)
@@ -111,7 +110,6 @@
     maybe_own(*send_y0(0), core == xh)
     for i in range(1, 4 * ny):
         remote(*send_y0(i))
-    lax.fori_loop(wide // 2, 2 * wide, send_x_step, 0)
 
     for one in loads[3:]:
         one.wait()
@@ -137,8 +135,18 @@
         second = jnp.dot(s_lo[...], table[:, 0:128], preferred_element_type=F32)
         return first[:, 0:128] + (first[:, 128:256] + second)
 
+    for p, (late, dy, rows) in enumerate(pieces):
+        wait(tq.at[p], recv, 14 + p)
+        for i in range(4):
+            x2 = (x + i) % 4
+            target = device((y + dy) % ny, x2, z, xh)
+            args = (tq.at[p, x2 % 2, x2 // 2], xr.at[place, :, rows], 1 + 12 * late, target)
+            if dy + i:
+                remote(*args, 11)
+            else:
+                maybe_own(*args, core == xh, 11)
     wait(yb, recv, 2)
-    wait(xr, recv, 1)
+    wait(xr.at[pl.ds(0, 2 * ny)], recv, 1)
     partner = device(y, x, z, 1 - core)
     halo = pl.ds(28 + 8 * core, 8)
     halo_copy = pltpu.make_async_remote_copy(
@@ -157,7 +165,8 @@
         return jnp.concatenate(parts, axis=0)
 
     def spread_group(i, carry):
-        group = (1 - core) * (3 - i) + core * i
+        turn = (i % 2) * 2 + i // 2
+        group = (1 - core) * (3 - turn) + core * turn
         for pair in range(4):
             parts = [split(level_x(group * 8 + 2 * pair + k)) for k in range(2)]
             rhs = jnp.concatenate(
@@ -181,7 +190,9 @@
 
         return carry
 
-    lax.fori_loop(0, 4, spread_group, 0)
+    lax.fori_loop(0, 2, spread_group, 0)
+    wait(xr.at[pl.ds(0, 2 * ny)], recv, 13)
+    lax.fori_loop(2, 4, spread_group, 0)
     halo_copy.wait()
 
     def column_g(level):
@@ -317,11 +328,10 @@
     curve = jnp.sum(total[1:2], axis=1, keepdims=True)
     scale_out[...] = jnp.broadcast_to(-(norm / (norm + curve)), (16, 128))
 
+    by_z = rp.reshape(nz, 4 * ny, 16, 128)
     wait(gcol, recv, 5)
-    some = 2 * wide - 1
-    xs_all = xr.reshape(2 * wide, 16, 128)
     for phase, all_of, but_one in (
-        (1, xs_all, xs_all.at[pl.ds(0, some)]),
+        (11, rp, rp.at[pl.ds(0, 4 * ny - 1)]),
         (2, yb, yb.at[pl.ds(0, 4 * ny - 1)]),
         (5, rp, rp.at[pl.ds(0, 4 * ny - 1)]),
         (6, rp, rp.at[pl.ds(0, 4 * ny - 1)]),
@@ -336,7 +346,7 @@
             wait(all_of, send, phase)
 
     for phase, ref, count in (
-        (0, zb, nz - 1), (3, rp, nz - 1), (4, rp, nz - 1), (8, rz, nz - 1), (9, slot_a, 2 * nz - 1), (10, slot_b, 4 * ny - 1)
+        (12, by_z, nz - 1), (0, zb, nz - 1), (3, rp, nz - 1), (4, rp, nz - 1), (8, rz, nz - 1), (9, slot_a, 2 * nz - 1), (10, slot_b, 4 * ny - 1)
     ):
         wait(ref.at[pl.ds(0, count)], send, phase)
 
@@ -376,6 +386,7 @@
             v32(72, wide, 128),
             v32(2 * ny, nz, 32, 128),
             v32(2, 2 * ny, nz, 16, 128),
+            v32(2 * ny, 2, 2, nz, 8, 128),
             v32(wide * 32, 128),
             v16(wide, 32, 128),
             v16(wide, 32, 128),
@@ -393,15 +404,14 @@
             v32(8, 128),
             v32(4 * ny, 8, 128),
             pltpu.SemaphoreType.DMA((5,)),
-            pltpu.SemaphoreType.DMA((11,)),
-            pltpu.SemaphoreType.DMA((11,)),
-            pltpu.SemaphoreType.REGULAR((1,)),
+            pltpu.SemaphoreType.DMA((13,)),
+            pltpu.SemaphoreType.DMA((14 + 2 * ny,)),
         ],
         compiler_params=pltpu.CompilerParams(
             has_side_effects=True, collective_id=0, vmem_limit_bytes=62 * 2**20
         ),
     )(
-        ensemble,
+        ensemble.reshape(2 * ny, nz, 2, lev, cols),
         innovation,
         obs_inverse,
         root_tiles,

time: 96.4 us -> 90.4 us (0.938)
  Pallas kernels: 92.7 us -> 86.7 us
    pallas_call x1, Pallas kernels: 92.7 us -> 86.7 us  [body(): pl.pallas_call(functools.partial(kernel, shape), out_shape=(jax.ShapeDtyp...]
where the time goes in v4:
time: 90.4 us; the launch traced here: 90.2 us
  Pallas kernels  86.7 us (96%)
  other arithmetic  2.9 us (3%)
    pallas_call x1, Pallas kernels, body(): pl.pallas_call(functools.partial(kernel, shape), out_shape=(jax.ShapeDtyp...  86.7 us
    mul x2, other arithmetic, body(): return ((gradient * scale).reshape(ensemble.shape), image * scale)  2.9 us

profile of v4, /device:TPU:1, one launch (start us, length us, event | category | flops | bytes accessed | tf_op | source)
XLA Modules:
  0.0 90.2 jit_solution(1094753810479995457)
XLA Ops:
  0.6 86.7 %shard_map.95 = (f32[64,2,16,128]{3,2,1,0:T(8,128)}, f32[16,128]{1,0:T(8,128)}, f32[16,128]{1,0:T(8,128)}) custom-call(f32[8,8,2,16,128]{4,3,2,1,0:T(8,128)} %bitcast.4, f32[16,128]{1,0:T(8,128)} %innov.1, f32[16,128]{1,0:T(8,128)} %obsinv.1, f32[8,128,128]{2,1,0:T(8,128)} %tiles_in.1, s32[8,64]{1,0:T(8,128)} %bitcast.6, s32[1,64]{1,0:T(1,128)} %bitcast.8, ...), custom_call_target="tpu_custom_call" | custom-call | tf_op jit(solution)/shard_map/pallas_call | solution.py:367
  87.3 0.0 copy-start
  87.3 0.0 copy-start.1
  87.3 2.3 %broadcast_multiply_fusion = f32[64,2,16,128]{3,2,1,0:T(8,128)} fusion(f32[64,2,16,128]{3,2,1,0:T(8,128)} %get-tuple-element.5, f32[16,128]{1,0:T(8,128)} %get-tuple-element.6), kind=kLoop, calls=%fused_computation | loop fusion | flops 262144 | bytes 2105344 | tf_op jit(solution)/shard_map/mul | solution.py:424
  89.6 0.0 copy-done
  89.6 0.0 copy-done.1
  89.6 0.6 mul.13
Async XLA Ops:
  87.3 2.3 %copy-start = (f32[16,128]{1,0:T(8,128)S(1)}, f32[16,128]{1,0:T(8,128)}, u32[]{:S(2)}) copy-start(f32[16,128]{1,0:T(8,128)} %get-tuple-element.6) | copy-start | bytes 24580
  87.3 2.3 %copy-start.1 = (f32[16,128]{1,0:T(8,128)S(1)}, f32[16,128]{1,0:T(8,128)}, u32[]{:S(2)}) copy-start(f32[16,128]{1,0:T(8,128)} %get-tuple-element.7) | copy-start | bytes 24580

commit v5 on v4

--- a/solution.py
+++ b/solution.py
@@ -211,25 +211,30 @@
         return norm + total * total
 
 
+    base = 14 + 2 * ny
+
     def along_z(q):
         half = pl.ds(16 * q, 16)
-        pltpu.make_async_copy(gs.at[:, z, half], tz.at[q, :, z], recv.at[3 + q]).start()
-        for i in range(1, nz):
-            z2 = (z + i) % nz
-            remote(gs.at[:, z2, half], tz.at[q, :, z], 3 + q, device(y, x, z2, core))
-
-    def within(q):
-        wait(tz.at[q], recv, 3 + q)
+        for dy in range(ny):
+            p = q * ny + dy
+            y2 = pl.ds(2 * ((y + dy) % ny), 2)
+            pltpu.make_async_copy(gs.at[y2, z, half], tz.at[p, :, z], recv.at[base + p]).start()
+            for i in range(1, nz):
+                z2 = (z + i) % nz
+                remote(gs.at[y2, z2, half], tz.at[p, :, z], base + p, device(y, x, z2, core), 3)
+
+    def within(q, turns):
         first = pl.ds((y * 2 + xl) * nz, nz)
-        for i in range(2 * ny):
-            y2 = (y + i // 2) % ny
-            xl2 = (xl + i % 2) % 2
-            target = device(y2, core * 2 + xl2, z, q)
-            args = (tz.at[q, y2 * 2 + xl2], gcol.at[first, xh], 5, target)
-            if i:
-                remote(*args)
-            else:
-                maybe_own(*args, (core == xh) & (core == q))
+        for dy in turns:
+            p = q * ny + dy
+            wait(tz.at[p], recv, base + p)
+            for i in range(2):
+                xl2 = (xl + i) % 2
+                args = (tz.at[p, xl2], gcol.at[first, xh], 5, device((y + dy) % ny, core * 2 + xl2, z, q))
+                if dy + i:
+                    remote(*args)
+                else:
+                    maybe_own(*args, (core == xh) & (core == q))
 
     norm = lax.fori_loop(0, 16, own_g, jnp.zeros((wide, 128), F32))
     along_z(0)
@@ -291,7 +296,7 @@
     maybe_own(*send_p(y, 0), core == xh)
     for k in range(1, 4):
         remote(*send_p(y, k))
-    within(0)
+    within(0, range(ny // 2))
     wait(rp, recv, 6)
     total = rp[0]
     for k in range(1, 4 * ny):
@@ -300,6 +305,8 @@
     for i in range(1, nz):
         remote(sz.at[(z + i) % nz], rz.at[z], 8, device(y, x, (z + i) % nz, core))
     rz[z] = sz[z]
+    within(0, range(ny // 2, ny))
+    within(1, range(ny // 2))
     wait(rz.at[pl.ds(0, nz - 1)], recv, 8)
     image = rz[0]
     for k in range(1, nz):
@@ -322,7 +329,7 @@
             total = total + dst[k]
         return total
 
-    part[...] = share(mine, slot_a, 9, z * 2 + core, 2 * nz, near, functools.partial(within, 1))
+    part[...] = share(mine, slot_a, 9, z * 2 + core, 2 * nz, near, functools.partial(within, 1, range(ny // 2, ny)))
     total = share(part, slot_b, 10, y * 4 + x, 4 * ny, far)
     norm = jnp.sum(total[0:1], axis=1, keepdims=True)
     curve = jnp.sum(total[1:2], axis=1, keepdims=True)
@@ -346,7 +353,7 @@
             wait(all_of, send, phase)
 
     for phase, ref, count in (
-        (12, by_z, nz - 1), (0, zb, nz - 1), (3, rp, nz - 1), (4, rp, nz - 1), (8, rz, nz - 1), (9, slot_a, 2 * nz - 1), (10, slot_b, 4 * ny - 1)
+        (12, by_z, nz - 1), (0, zb, nz - 1), (3, by_z, nz - 1), (8, rz, nz - 1), (9, slot_a, 2 * nz - 1), (10, slot_b, 4 * ny - 1)
     ):
         wait(ref.at[pl.ds(0, count)], send, phase)
 
@@ -385,7 +392,7 @@
             v32(72, wide, 128),
             v32(72, wide, 128),
             v32(2 * ny, nz, 32, 128),
-            v32(2, 2 * ny, nz, 16, 128),
+            v32(2 * ny, 2, nz, 16, 128),
             v32(2 * ny, 2, 2, nz, 8, 128),
             v32(wide * 32, 128),
             v16(wide, 32, 128),
@@ -405,7 +412,7 @@
             v32(4 * ny, 8, 128),
             pltpu.SemaphoreType.DMA((5,)),
             pltpu.SemaphoreType.DMA((13,)),
-            pltpu.SemaphoreType.DMA((14 + 2 * ny,)),
+            pltpu.SemaphoreType.DMA((14 + 4 * ny,)),
         ],
         compiler_params=pltpu.CompilerParams(
             has_side_effects=True, collective_id=0, vmem_limit_bytes=62 * 2**20

time: 90.4 us -> 90 us (level)
  no operation moved by 1% of the time
where the time goes in v5:
time: 90 us; the launch traced here: 89.9 us
  Pallas kernels  86.3 us (96%)
  other arithmetic  2.9 us (3%)
    pallas_call x1, Pallas kernels, body(): pl.pallas_call(functools.partial(kernel, shape), out_shape=(jax.ShapeDtyp...  86.3 us
    mul x2, other arithmetic, body(): return ((gradient * scale).reshape(ensemble.shape), image * scale)  2.9 us

profile of v5, /device:TPU:1, one launch (start us, length us, event | category | flops | bytes accessed | tf_op | source)
XLA Modules:
  0.0 89.9 jit_solution(589847386258380084)
XLA Ops:
  0.6 86.3 %shard_map.95 = (f32[64,2,16,128]{3,2,1,0:T(8,128)}, f32[16,128]{1,0:T(8,128)}, f32[16,128]{1,0:T(8,128)}) custom-call(f32[8,8,2,16,128]{4,3,2,1,0:T(8,128)} %bitcast.4, f32[16,128]{1,0:T(8,128)} %innov.1, f32[16,128]{1,0:T(8,128)} %obsinv.1, f32[8,128,128]{2,1,0:T(8,128)} %tiles_in.1, s32[8,64]{1,0:T(8,128)} %bitcast.6, s32[1,64]{1,0:T(1,128)} %bitcast.8, ...), custom_call_target="tpu_custom_call" | custom-call | tf_op jit(solution)/shard_map/pallas_call | solution.py:374
  86.9 0.0 copy-start
  87.0 0.0 copy-start.1
  87.0 2.3 %broadcast_multiply_fusion = f32[64,2,16,128]{3,2,1,0:T(8,128)} fusion(f32[64,2,16,128]{3,2,1,0:T(8,128)} %get-tuple-element.5, f32[16,128]{1,0:T(8,128)} %get-tuple-element.6), kind=kLoop, calls=%fused_computation | loop fusion | flops 262144 | bytes 2105344 | tf_op jit(solution)/shard_map/mul | solution.py:431
  89.3 0.0 copy-done
  89.3 0.0 copy-done.1
  89.3 0.6 mul.13
Async XLA Ops:
  86.9 2.3 %copy-start = (f32[16,128]{1,0:T(8,128)S(1)}, f32[16,128]{1,0:T(8,128)}, u32[]{:S(2)}) copy-start(f32[16,128]{1,0:T(8,128)} %get-tuple-element.6) | copy-start | bytes 24580
  87.0 2.3 %copy-start.1 = (f32[16,128]{1,0:T(8,128)S(1)}, f32[16,128]{1,0:T(8,128)}, u32[]{:S(2)}) copy-start(f32[16,128]{1,0:T(8,128)} %get-tuple-element.7) | copy-start | bytes 24580

commit v6 on v5

--- a/solution.py
+++ b/solution.py
@@ -311,7 +311,6 @@
     image = rz[0]
     for k in range(1, nz):
         image = image + rz[k]
-    image_out[...] = image
 
     curve = jnp.sum(weight * image * image, axis=0, keepdims=True)
     norm = jnp.sum(norm, axis=0, keepdims=True)
@@ -333,7 +332,9 @@
     total = share(part, slot_b, 10, y * 4 + x, 4 * ny, far)
     norm = jnp.sum(total[0:1], axis=1, keepdims=True)
     curve = jnp.sum(total[1:2], axis=1, keepdims=True)
-    scale_out[...] = jnp.broadcast_to(-(norm / (norm + curve)), (16, 128))
+    scale = jnp.broadcast_to(-(norm / (norm + curve)), (16, 128))
+    scale_out[...] = scale
+    image_out[...] = scale * image
 
     by_z = rp.reshape(nz, 4 * ny, 16, 128)
     wait(gcol, recv, 5)
@@ -428,7 +429,7 @@
         member_weight,
         col_index.T,
     )
-    return (gradient * scale).reshape(ensemble.shape), image * scale
+    return (gradient * scale).reshape(ensemble.shape), image
 
 
 def solution(mesh):

time: 90 us -> 89.9 us (level)
    mul x2 -> x1, other arithmetic: 2.9 us -> 2.29 us  [body(): return ((gradient * scale).reshape(ensemble.shape), image)]
where the time goes in v6:
time: 89.9 us; the launch traced here: 89.6 us
  Pallas kernels  86 us (96%)
  other arithmetic  2.29 us (3%)
    pallas_call x1, Pallas kernels, body(): pl.pallas_call(functools.partial(kernel, shape), out_shape=(jax.ShapeDtyp...  86 us
    mul x1, other arithmetic, body(): return ((gradient * scale).reshape(ensemble.shape), image)  2.29 us

profile of v6, /device:TPU:1, one launch (start us, length us, event | category | flops | bytes accessed | tf_op | source)
XLA Modules:
  0.0 89.6 jit_solution(9765210797861112890)
XLA Ops:
  0.6 86.0 %shard_map.95 = (f32[64,2,16,128]{3,2,1,0:T(8,128)}, f32[16,128]{1,0:T(8,128)}, f32[16,128]{1,0:T(8,128)}) custom-call(f32[8,8,2,16,128]{4,3,2,1,0:T(8,128)} %bitcast.4, f32[16,128]{1,0:T(8,128)} %innov.1, f32[16,128]{1,0:T(8,128)} %obsinv.1, f32[8,128,128]{2,1,0:T(8,128)} %tiles_in.1, s32[8,64]{1,0:T(8,128)} %bitcast.6, s32[1,64]{1,0:T(1,128)} %bitcast.8, ...), custom_call_target="tpu_custom_call" | custom-call | tf_op jit(solution)/shard_map/pallas_call | solution.py:375
  86.7 0.0 copy-start
  86.7 2.3 %broadcast_multiply_fusion = f32[64,2,16,128]{3,2,1,0:T(8,128)} fusion(f32[64,2,16,128]{3,2,1,0:T(8,128)} %get-tuple-element.5, f32[16,128]{1,0:T(8,128)} %get-tuple-element.6), kind=kLoop, calls=%fused_computation | loop fusion | flops 262144 | bytes 2105344 | tf_op jit(solution)/shard_map/mul | solution.py:432
  89.0 0.0 copy-done
  89.0 0.6 copy.11
Async XLA Ops:
  86.7 2.3 %copy-start = (f32[16,128]{1,0:T(8,128)S(1)}, f32[16,128]{1,0:T(8,128)}, u32[]{:S(2)}) copy-start(f32[16,128]{1,0:T(8,128)} %get-tuple-element.11) | copy-start | bytes 24580
